TPU v7x, 32 devices: a whole 2x2x4 slice. The times are simulated.
32 devices in a mesh: grain: 8 (over z, y), cell: 4 (over x, core).
Axes of the slice: x: 2, y: 2, z: 4, core: 2. Of those that a mesh axis runs over, the one named last changes fastest.
Arguments:
- displacement: float32 [1024, 3, 768], P(('grain', 'cell')), may hold values from -0.1 to 0.1
- velocity: float32 [1024, 3, 768], P(('grain', 'cell')), may hold values from -6 to 6
- centers: float32 [3, 1024], P(None, ('grain', 'cell')), may hold values from -4 to 4
- tile_list: int32 [1024, 4, 2], P(('grain', 'cell')), may hold values from 0 to 5
- broken_bits: int32 [1024, 4, 2048], P(('grain', 'cell')), may hold values from 0 to 255, as said below
- surface_nodes: int32 [1024, 512], P(('grain', 'cell')), may hold values from 0 to 767, as said below
- send_order: int32 [32, 128], P(('grain', 'cell')), may hold values from 0 to 127, each once within a row
- pair_list: int32 [32, 128, 2], P(('grain', 'cell')), may hold values from 0 to 127
- pair_count: int32 [32], P(('grain', 'cell')), may hold values from 1 to 128, 2048 in all
Outputs:
- force: float32 [1024, 3, 768], P(('grain', 'cell'))
- new_velocity: float32 [1024, 3, 768], P(('grain', 'cell'))
Inputs may be any that keep to these rules, and one draw needn't show every extreme that they name: `surface_nodes`: within a grain the 512 surface node indices are distinct. `send_order`: each row is a permutation of the device's 128 surface blocks; position p goes to device p div 4, so every device receives exactly 4 blocks from each device. `broken_bits`: each word packs 8 broken flags, any bit pattern.
All inputs are finite; a program needn't handle non-finite values. No bound on the sum of `pair_count` on one device may be relied on, other than what follows from the above.
Results may differ from a plain program's by a relative error of at most 0.0003.
Values sent between devices are 32-bit elements; how exact they have to be, the bound alone decides.
A program may use at most 64 MiB of HBM per device.

v0:
```python
import jax
import jax.numpy as jnp
from jax import lax
from jax.sharding import PartitionSpec as P

BLK = 128
SB = 4


HORIZON = 3.0
BOND_STIFF = 5.0
CONTACT_STIFF = 0.02
CONTACT_DAMP = 0.05
CONTACT_RANGE = 9.0
TIME_STEP = 0.5


def lattice(node_count):
    node_index = jnp.arange(node_count, dtype=jnp.int32)
    return jnp.stack([node_index % 8, node_index // 8 % 8, node_index // 64]).astype(jnp.float32)


def unpack(bit_words):
    shifts = jnp.arange(8, dtype=jnp.int32)
    bit_table = jnp.right_shift(bit_words[:, None], shifts[None, :]) & 1
    return bit_table.reshape(BLK, BLK)


def bond_tile(rest_grid, now_grid, tile_pair, tile_words):
    row_start = tile_pair[0] * BLK
    col_start = tile_pair[1] * BLK
    rest_rows = lax.dynamic_slice_in_dim(rest_grid, row_start, BLK, 1)
    rest_cols = lax.dynamic_slice_in_dim(rest_grid, col_start, BLK, 1)
    now_rows = lax.dynamic_slice_in_dim(now_grid, row_start, BLK, 1)
    now_cols = lax.dynamic_slice_in_dim(now_grid, col_start, BLK, 1)
    rest_gap = rest_cols[:, None, :] - rest_rows[:, :, None]
    rest_len = jnp.sqrt(jnp.sum(rest_gap * rest_gap, axis=0))
    now_gap = now_cols[:, None, :] - now_rows[:, :, None]
    now_len = jnp.sqrt(jnp.sum(now_gap * now_gap, axis=0))
    live_bond = (rest_len > 0.5) & (rest_len <= HORIZON) & (unpack(tile_words) == 0)
    safe_rest = jnp.where(live_bond, rest_len, 1.0)
    safe_now = jnp.where(live_bond, now_len, 1.0)
    coefficient = jnp.where(
        live_bond, BOND_STIFF * (now_len - rest_len) / (safe_rest * safe_now), 0.0
    )
    return jnp.sum(coefficient[None] * now_gap, axis=2)


def grain_bonds(displacement, tile_list, bit_words):
    rest_grid = lattice(displacement.shape[1])
    now_grid = rest_grid + displacement

    def tile_step(force_sum, entry_item):
        tile_pair, tile_words = entry_item
        tile_force = bond_tile(rest_grid, now_grid, tile_pair, tile_words)
        row_start = tile_pair[0] * BLK
        old_rows = lax.dynamic_slice_in_dim(force_sum, row_start, BLK, 1)
        return (
            lax.dynamic_update_slice_in_dim(force_sum, old_rows + tile_force, row_start, 1),
            None,
        )

    force_sum, _ = lax.scan(tile_step, jnp.zeros_like(displacement), (tile_list, bit_words))
    return force_sum


def bonds_all(displacement, tile_list, bit_words):
    grains = displacement.shape[0]

    def grouped(array):
        return array.reshape((grains // 16, 16) + array.shape[1:])

    def group_step(entry_item):
        return jax.vmap(grain_bonds)(*entry_item)

    forces = lax.map(group_step, (grouped(displacement), grouped(tile_list), grouped(bit_words)))
    return forces.reshape(displacement.shape)


def contact_pair(left_block, right_block):
    gap_vec = left_block[:3, :, None] - right_block[:3, None, :]
    slip_vec = left_block[3:, :, None] - right_block[3:, None, :]
    weights = jnp.exp(-jnp.sum(gap_vec * gap_vec, axis=0) / CONTACT_RANGE)
    push_term = weights[None] * (CONTACT_STIFF * gap_vec - CONTACT_DAMP * slip_vec)
    return (jnp.sum(push_term, axis=2), -jnp.sum(push_term, axis=1))


def surface_blocks(displacement, velocity, centers, surface_nodes):
    rest_grid = lattice(displacement.shape[2])
    now_grid = rest_grid[None] + displacement + centers.T[:, :, None]
    full_state = jnp.concatenate([now_grid, velocity], axis=1)
    picked = jnp.take_along_axis(full_state, surface_nodes[:, None, :], axis=2)
    grains = picked.shape[0]
    return picked.reshape(grains, 6, SB, BLK).transpose(0, 2, 1, 3).reshape(grains * SB, 6, BLK)


def spread_surface(block_force, surface_nodes, node_count):
    grains = surface_nodes.shape[0]
    surface_force = (
        block_force.reshape(grains, SB, 3, BLK).transpose(0, 2, 1, 3).reshape(grains, 3, SB * BLK)
    )

    def one_grain(node_ids, node_force):
        return jnp.zeros((3, node_count), node_force.dtype).at[:, node_ids].add(node_force)

    return jax.vmap(one_grain)(surface_nodes, surface_force)


def add_pairs(accumulated, blocks, chosen, in_range):
    left_force, right_force = jax.vmap(contact_pair)(blocks[chosen[:, 0]], blocks[chosen[:, 1]])
    live_mask = in_range.astype(jnp.float32)[:, None, None]
    accumulated = accumulated.at[chosen[:, 0]].add(left_force * live_mask)
    return accumulated.at[chosen[:, 1]].add(right_force * live_mask)


def on_device(
    displacement,
    velocity,
    centers,
    tile_list,
    broken_bits,
    surface_nodes,
    send_order,
    pair_list,
    pair_count,
):
    grain_count = lax.axis_size("grain")
    cell_count = lax.axis_size("cell")
    owner_count = grain_count * cell_count
    blocks = surface_blocks(displacement, velocity, centers, surface_nodes)
    send_index = send_order[0]
    outgoing = blocks[send_index]
    slot_count = outgoing.shape[0]
    per_peer = slot_count // owner_count
    received = lax.all_to_all(
        outgoing.reshape(owner_count, per_peer, 6, BLK),
        ("grain", "cell"),
        split_axis=0,
        concat_axis=0,
        tiled=True,
    )
    received = received.reshape(slot_count, 6, BLK)
    bond_force = bonds_all(displacement, tile_list, broken_bits)
    batch_size = 32
    pair_total = pair_count[0]
    own_pairs = pair_list[0]
    round_count = (pair_total + batch_size - 1) // batch_size

    def own_round(round_index, accumulated):
        flat_index = round_index * batch_size + jnp.arange(batch_size, dtype=jnp.int32)
        in_range = flat_index < pair_total
        chosen = own_pairs[jnp.where(in_range, flat_index, 0)]
        return add_pairs(accumulated, received, chosen, in_range)

    slot_force = lax.fori_loop(
        0, round_count, own_round, jnp.zeros((slot_count, 3, BLK), jnp.float32)
    )
    returned = lax.all_to_all(
        slot_force.reshape(owner_count, per_peer, 3, BLK),
        ("grain", "cell"),
        split_axis=0,
        concat_axis=0,
        tiled=True,
    )
    returned = returned.reshape(slot_count, 3, BLK)
    block_force = jnp.zeros((slot_count, 3, BLK), jnp.float32).at[send_index].set(returned)
    contact_force = spread_surface(block_force, surface_nodes, displacement.shape[2])
    force = bond_force + contact_force
    return (force, velocity + TIME_STEP * force)


def solution(mesh):
    return jax.shard_map(
        on_device,
        mesh=mesh,
        in_specs=(
            P(("grain", "cell"), None, None),
            P(("grain", "cell"), None, None),
            P(None, ("grain", "cell")),
            P(("grain", "cell"), None, None),
            P(("grain", "cell"), None, None),
            P(("grain", "cell"), None),
            P(("grain", "cell"), None),
            P(("grain", "cell"), None, None),
            P(("grain", "cell")),
        ),
        out_specs=(P(("grain", "cell"), None, None), P(("grain", "cell"), None, None)),
        check_vma=False,
    )
```

profile of v0, /device:TPU:1, one launch (start us, length us, event | category | flops | bytes accessed | tf_op | source)
XLA Modules:
  0.0 1880.7 jit_solution(12858217277745281307)
XLA Ops:
  11.9 236.8 %gather_fusion.7 = f32[16384,6]{1,0:T(8,128)} fusion(f32[32,6,768]{1,2,0:T(8,128)} %copy.129, s32[16384]{0:T(1024)S(1)} %bitcast.114), kind=kCustom, calls=%fused_computation.7 | custom fusion | bytes 917504 | tf_op jit(solution)/shard_map/jit(take_along_axis)/gather | solution.py:92
  263.3 1431.0 %while.55 = (s32[]{:T(128)}, f32[2,16,3,768]{3,2,1,0:T(4,128)}, s32[2,16,4,2]{1,0,3,2:T(2,128)S(1)}, s32[2,16,4,2048]{3,2,1,0:T(4,128)}, f32[2,16,3,768]{3,1,0,2...) while((s32[]{:T(128)}, f32[2,16,3,768]{3,2,1,0:T(4,128)}, ...), condition=%wide.region_7.8_spmd, body=%wide.region_0.7_spmd.sunk | while | flops 10291949 | bytes 15364759 | solution.py:76
  279.2 698.8 %while.57 = (s32[]{:T(128)}, f32[16,3,768]{2,1,0:T(4,128)S(1)}, s32[4,16,2]{1,0,2:T(4,128)S(1)}, f32[3,768]{1,0:T(4,128)S(1)}, s32[4,16,2048]{1,2,0:T(8,128)}, /...) while((s32[]{:T(128)}, f32[16,3,768]{2,1,0:T(4,128)S(1)}, ...), condition=%wide.region_6.6_spmd, body=%wide.region_1.5_spmd.sunk | while | flops 10224363 | bytes 11833694 | solution.py:63
  279.5 19.1 %while.58 = (s32[]{:T(128)}, f32[3,768]{1,0:T(4,128)S(1)}, s32[16,2]{0,1:T(2,128)S(1)}, f32[16,3,128]{2,1,0:T(4,128)S(1)}, s32[]{:T(128)}) while((s32[]{:T(128)}, f32[3,768]{1,0:T(4,128)S(1)}, s32[16,2]{0,1:T(2,128)S(1)}, f32[16,3,128]{2,1,0:T(4,128)S(1)}, s32[]{:T(128)}) %tuple.168), condition=%wide.while_cond.1, body=%wide.while_body.1.sunk | while | flops 2 | bytes 4201 | solution.py:32
  298.6 20.6 %while.59 = (s32[]{:T(128)}, f32[3,768]{1,0:T(4,128)S(1)}, s32[16,2]{0,1:T(2,128)S(1)}, f32[16,3,128]{2,1,0:T(4,128)S(1)}, s32[]{:T(128)}) while((s32[]{:T(128)}, f32[3,768]{1,0:T(4,128)S(1)}, s32[16,2]{0,1:T(2,128)S(1)}, f32[16,3,128]{2,1,0:T(4,128)S(1)}, s32[]{:T(128)}) %tuple.187), condition=%wide.while_cond, body=%wide.while_body.sunk | while | flops 2 | bytes 4201 | solution.py:33
  351.2 102.8 %while.60 = (s32[]{:T(128)}, f32[16,3,768]{2,1,0:T(4,128)S(1)}, s32[16,3]{0,1:T(4,128)S(1)}, f32[16,3,128]{2,1,0:T(4,128)S(1)}, s32[]{:T(128)}, /*index=5*/s32[3]{0:T(128)S(1)}, s32[]{:T(128)}) while((s32[]{:T(128)}, f32[16,3,768]{2,1,0:T(4,128)S(1)}, s32[16,3]{0,1:T(4,128)S(1)}, f32[16,3,128]{2,1,0:T(4,128)S(1)}, s32[]{:T(128)}, ...), condition=%wide.while_cond.2, body=%wide.while_body.2.sunk | while | flops 403 | bytes 7859 | solution.py:59
  473.3 20.6 %while.59 = (s32[]{:T(128)}, f32[3,768]{1,0:T(4,128)S(1)}, s32[16,2]{0,1:T(2,128)S(1)}, f32[16,3,128]{2,1,0:T(4,128)S(1)}, s32[]{:T(128)}) while((s32[]{:T(128)}, f32[3,768]{1,0:T(4,128)S(1)}, s32[16,2]{0,1:T(2,128)S(1)}, f32[16,3,128]{2,1,0:T(4,128)S(1)}, s32[]{:T(128)}) %tuple.187), condition=%wide.while_cond, body=%wide.while_body.sunk | while | flops 2 | bytes 4201 | solution.py:33
  525.9 102.7 %while.60 = (s32[]{:T(128)}, f32[16,3,768]{2,1,0:T(4,128)S(1)}, s32[16,3]{0,1:T(4,128)S(1)}, f32[16,3,128]{2,1,0:T(4,128)S(1)}, s32[]{:T(128)}, /*index=5*/s32[3]{0:T(128)S(1)}, s32[]{:T(128)}) while((s32[]{:T(128)}, f32[16,3,768]{2,1,0:T(4,128)S(1)}, s32[16,3]{0,1:T(4,128)S(1)}, f32[16,3,128]{2,1,0:T(4,128)S(1)}, s32[]{:T(128)}, ...), condition=%wide.while_cond.2, body=%wide.while_body.2.sunk | while | flops 403 | bytes 7859 | solution.py:59
  648.0 20.6 %while.59 = (s32[]{:T(128)}, f32[3,768]{1,0:T(4,128)S(1)}, s32[16,2]{0,1:T(2,128)S(1)}, f32[16,3,128]{2,1,0:T(4,128)S(1)}, s32[]{:T(128)}) while((s32[]{:T(128)}, f32[3,768]{1,0:T(4,128)S(1)}, s32[16,2]{0,1:T(2,128)S(1)}, f32[16,3,128]{2,1,0:T(4,128)S(1)}, s32[]{:T(128)}) %tuple.187), condition=%wide.while_cond, body=%wide.while_body.sunk | while | flops 2 | bytes 4201 | solution.py:33
  700.6 102.7 %while.60 = (s32[]{:T(128)}, f32[16,3,768]{2,1,0:T(4,128)S(1)}, s32[16,3]{0,1:T(4,128)S(1)}, f32[16,3,128]{2,1,0:T(4,128)S(1)}, s32[]{:T(128)}, /*index=5*/s32[3]{0:T(128)S(1)}, s32[]{:T(128)}) while((s32[]{:T(128)}, f32[16,3,768]{2,1,0:T(4,128)S(1)}, s32[16,3]{0,1:T(4,128)S(1)}, f32[16,3,128]{2,1,0:T(4,128)S(1)}, s32[]{:T(128)}, ...), condition=%wide.while_cond.2, body=%wide.while_body.2.sunk | while | flops 403 | bytes 7859 | solution.py:59
  822.7 20.6 %while.59 = (s32[]{:T(128)}, f32[3,768]{1,0:T(4,128)S(1)}, s32[16,2]{0,1:T(2,128)S(1)}, f32[16,3,128]{2,1,0:T(4,128)S(1)}, s32[]{:T(128)}) while((s32[]{:T(128)}, f32[3,768]{1,0:T(4,128)S(1)}, s32[16,2]{0,1:T(2,128)S(1)}, f32[16,3,128]{2,1,0:T(4,128)S(1)}, s32[]{:T(128)}) %tuple.187), condition=%wide.while_cond, body=%wide.while_body.sunk | while | flops 2 | bytes 4201 | solution.py:33
  875.3 102.7 %while.60 = (s32[]{:T(128)}, f32[16,3,768]{2,1,0:T(4,128)S(1)}, s32[16,3]{0,1:T(4,128)S(1)}, f32[16,3,128]{2,1,0:T(4,128)S(1)}, s32[]{:T(128)}, /*index=5*/s32[3]{0:T(128)S(1)}, s32[]{:T(128)}) while((s32[]{:T(128)}, f32[16,3,768]{2,1,0:T(4,128)S(1)}, s32[16,3]{0,1:T(4,128)S(1)}, f32[16,3,128]{2,1,0:T(4,128)S(1)}, s32[]{:T(128)}, ...), condition=%wide.while_cond.2, body=%wide.while_body.2.sunk | while | flops 403 | bytes 7859 | solution.py:59
  994.7 698.9 %while.57 = (s32[]{:T(128)}, f32[16,3,768]{2,1,0:T(4,128)S(1)}, s32[4,16,2]{1,0,2:T(4,128)S(1)}, f32[3,768]{1,0:T(4,128)S(1)}, s32[4,16,2048]{1,2,0:T(8,128)}, /...) while((s32[]{:T(128)}, f32[16,3,768]{2,1,0:T(4,128)S(1)}, ...), condition=%wide.region_6.6_spmd, body=%wide.region_1.5_spmd.sunk | while | flops 10224363 | bytes 11833694 | solution.py:63
  1014.0 20.6 %while.59 = (s32[]{:T(128)}, f32[3,768]{1,0:T(4,128)S(1)}, s32[16,2]{0,1:T(2,128)S(1)}, f32[16,3,128]{2,1,0:T(4,128)S(1)}, s32[]{:T(128)}) while((s32[]{:T(128)}, f32[3,768]{1,0:T(4,128)S(1)}, s32[16,2]{0,1:T(2,128)S(1)}, f32[16,3,128]{2,1,0:T(4,128)S(1)}, s32[]{:T(128)}) %tuple.187), condition=%wide.while_cond, body=%wide.while_body.sunk | while | flops 2 | bytes 4201 | solution.py:33
  1066.6 102.8 %while.60 = (s32[]{:T(128)}, f32[16,3,768]{2,1,0:T(4,128)S(1)}, s32[16,3]{0,1:T(4,128)S(1)}, f32[16,3,128]{2,1,0:T(4,128)S(1)}, s32[]{:T(128)}, /*index=5*/s32[3]{0:T(128)S(1)}, s32[]{:T(128)}) while((s32[]{:T(128)}, f32[16,3,768]{2,1,0:T(4,128)S(1)}, s32[16,3]{0,1:T(4,128)S(1)}, f32[16,3,128]{2,1,0:T(4,128)S(1)}, s32[]{:T(128)}, ...), condition=%wide.while_cond.2, body=%wide.while_body.2.sunk | while | flops 403 | bytes 7859 | solution.py:59
  1188.8 20.6 %while.59 = (s32[]{:T(128)}, f32[3,768]{1,0:T(4,128)S(1)}, s32[16,2]{0,1:T(2,128)S(1)}, f32[16,3,128]{2,1,0:T(4,128)S(1)}, s32[]{:T(128)}) while((s32[]{:T(128)}, f32[3,768]{1,0:T(4,128)S(1)}, s32[16,2]{0,1:T(2,128)S(1)}, f32[16,3,128]{2,1,0:T(4,128)S(1)}, s32[]{:T(128)}) %tuple.187), condition=%wide.while_cond, body=%wide.while_body.sunk | while | flops 2 | bytes 4201 | solution.py:33
  1241.4 102.8 %while.60 = (s32[]{:T(128)}, f32[16,3,768]{2,1,0:T(4,128)S(1)}, s32[16,3]{0,1:T(4,128)S(1)}, f32[16,3,128]{2,1,0:T(4,128)S(1)}, s32[]{:T(128)}, /*index=5*/s32[3]{0:T(128)S(1)}, s32[]{:T(128)}) while((s32[]{:T(128)}, f32[16,3,768]{2,1,0:T(4,128)S(1)}, s32[16,3]{0,1:T(4,128)S(1)}, f32[16,3,128]{2,1,0:T(4,128)S(1)}, s32[]{:T(128)}, ...), condition=%wide.while_cond.2, body=%wide.while_body.2.sunk | while | flops 403 | bytes 7859 | solution.py:59
  1363.5 20.6 %while.59 = (s32[]{:T(128)}, f32[3,768]{1,0:T(4,128)S(1)}, s32[16,2]{0,1:T(2,128)S(1)}, f32[16,3,128]{2,1,0:T(4,128)S(1)}, s32[]{:T(128)}) while((s32[]{:T(128)}, f32[3,768]{1,0:T(4,128)S(1)}, s32[16,2]{0,1:T(2,128)S(1)}, f32[16,3,128]{2,1,0:T(4,128)S(1)}, s32[]{:T(128)}) %tuple.187), condition=%wide.while_cond, body=%wide.while_body.sunk | while | flops 2 | bytes 4201 | solution.py:33
  1416.1 102.7 %while.60 = (s32[]{:T(128)}, f32[16,3,768]{2,1,0:T(4,128)S(1)}, s32[16,3]{0,1:T(4,128)S(1)}, f32[16,3,128]{2,1,0:T(4,128)S(1)}, s32[]{:T(128)}, /*index=5*/s32[3]{0:T(128)S(1)}, s32[]{:T(128)}) while((s32[]{:T(128)}, f32[16,3,768]{2,1,0:T(4,128)S(1)}, s32[16,3]{0,1:T(4,128)S(1)}, f32[16,3,128]{2,1,0:T(4,128)S(1)}, s32[]{:T(128)}, ...), condition=%wide.while_cond.2, body=%wide.while_body.2.sunk | while | flops 403 | bytes 7859 | solution.py:59
  1538.2 20.6 %while.59 = (s32[]{:T(128)}, f32[3,768]{1,0:T(4,128)S(1)}, s32[16,2]{0,1:T(2,128)S(1)}, f32[16,3,128]{2,1,0:T(4,128)S(1)}, s32[]{:T(128)}) while((s32[]{:T(128)}, f32[3,768]{1,0:T(4,128)S(1)}, s32[16,2]{0,1:T(2,128)S(1)}, f32[16,3,128]{2,1,0:T(4,128)S(1)}, s32[]{:T(128)}) %tuple.187), condition=%wide.while_cond, body=%wide.while_body.sunk | while | flops 2 | bytes 4201 | solution.py:33
  1590.8 102.8 %while.60 = (s32[]{:T(128)}, f32[16,3,768]{2,1,0:T(4,128)S(1)}, s32[16,3]{0,1:T(4,128)S(1)}, f32[16,3,128]{2,1,0:T(4,128)S(1)}, s32[]{:T(128)}, /*index=5*/s32[3]{0:T(128)S(1)}, s32[]{:T(128)}) while((s32[]{:T(128)}, f32[16,3,768]{2,1,0:T(4,128)S(1)}, s32[16,3]{0,1:T(4,128)S(1)}, f32[16,3,128]{2,1,0:T(4,128)S(1)}, s32[]{:T(128)}, ...), condition=%wide.while_cond.2, body=%wide.while_body.2.sunk | while | flops 403 | bytes 7859 | solution.py:59
  1697.3 47.3 %while.56 = (s32[]{:T(128)}, f32[128,3,128]{2,1,0:T(4,128)S(1)}, s32[]{:T(128)}, s32[]{:T(128)}, s32[128,2]{1,0:T(8,128)S(1)}, /*index=5*/f32[128,6,128]{2,1,0:T(8,128)S(1)}, s32[]{:T(128)}, s32[]{:T(128)}) while((s32[]{:T(128)}, f32[128,3,128]{2,1,0:T(4,128)S(1)}, s32[]{:T(128)}, s32[]{:T(128)}, s32[128,2]{1,0:T(8,128)S(1)}, ...), condition=%wide.region_14.15_spmd, body=%wide.region_8.14_spmd.sunk | while | flops 17866212 | bytes 10074609 | solution.py:155
  1745.3 20.4 %all-to-all-start.1 = ((f32[32,4,3,128]{3,1,2,0:T(4,128)}), f32[32,4,3,128]{3,1,2,0:T(4,128)S(1)}, u32[]{:S(2)}, u32[]{:S(2)}) async-start(f32[32,4,3,128]{3,1,2,0:T(4,128)} %copy.135), calls=%async_computation.1 | async-start | bytes 393216 | tf_op jit(solution)/shard_map/all_to_all | solution.py:158
  1784.3 87.9 %scatter_fusion.3 = f32[3,24576]{0,1:T(8,128)} fusion(f32[3,24576]{0,1:T(8,128)} %bitcast.116, s32[16384]{0:T(1024)S(1)} %bitcast.132, f32[16384,3]{1,0:T(8,128)} %bitcast.119), kind=kCustom, calls=%fused_computation.11 | custom fusion | flops 49152 | bytes 655360
  (1761 shorter events, 1662.2 us)
Async XLA Ops:
  3.1 8.9 copy-start.5
  248.7 14.5 copy-start.4
  248.7 14.6 copy-start
  256.0 1439.9 %all-to-all-start = ((f32[32,4,6,128]{3,1,2,0:T(4,128)}), f32[32,4,6,128]{3,1,2,0:T(4,128)}, u32[]{:S(2)}, u32[]{:S(2)}) async-start(f32[32,4,6,128]{3,1,2,0:T(4,128)} %copy.131), calls=%async_computation | async-start | bytes 786432 | tf_op jit(solution)/shard_map/all_to_all | solution.py:135
  263.3 1431.7 %copy-start.7 = (s32[1,128,2]{1,2,0:T(2,128)S(1)}, s32[1,128,2]{1,2,0:T(2,128)}, u32[]{:S(2)}) copy-start(s32[1,128,2]{1,2,0:T(2,128)} %param.22) | copy-start | bytes 3076
  1697.3 68.5 %copy-start.9 = (s32[2]{0:T(128)S(1)}, s32[2]{0:T(128)}, u32[]{:S(2)}) copy-start(s32[2]{0:T(128)} %constant.252) | copy-start | bytes 28
  1697.3 68.5 %copy-start.8 = (s32[2]{0:T(128)S(1)}, s32[2]{0:T(128)}, u32[]{:S(2)}) copy-start(s32[2]{0:T(128)} %constant.255) | copy-start | bytes 28
  1697.3 68.7 %copy-start.3 = (f32[2,16,3,768]{3,2,1,0:T(4,128)S(1)}, f32[2,16,3,768]{3,2,1,0:T(4,128)}, u32[]{:S(2)}) copy-start(f32[2,16,3,768]{3,2,1,0:T(4,128)} %get-tuple-element.825) | copy-start | bytes 884740
  1745.3 29.6 %all-to-all-start.1 = ((f32[32,4,3,128]{3,1,2,0:T(4,128)}), f32[32,4,3,128]{3,1,2,0:T(4,128)S(1)}, u32[]{:S(2)}, u32[]{:S(2)}) async-start(f32[32,4,3,128]{3,1,2,0:T(4,128)} %copy.135), calls=%async_computation.1 | async-start | bytes 393216 | tf_op jit(solution)/shard_map/all_to_all | solution.py:158
  1766.0 9.2 copy-start.6
  1872.3 7.7 copy-start.2
  1879.9 0.8 copy-start.1
where the time goes:
time: 1900 us; the launch traced here: 1880 us
  local copies, waits for them, and re-layouts  1080 us (57%)
  other arithmetic  761 us (40%)
  starting transfers between devices  27.6 us (1%)
    scatter x256, other arithmetic  562 us
    gather x768, local copies, waits for them, and re-layouts  317 us
    scatter x384, local copies, waits for them, and re-layouts  257 us
    gather x2, local copies, waits for them, and re-layouts, surface_blocks(): picked = jnp.take_along_axis(full_state, surface_nodes[:, None, :], axis=2)  242 us
    unnamed x5, other arithmetic  89 us
    shift_right_arithmetic x40, local copies, waits for them, and re-layouts, unpack(): bit_table = jnp.right_shift(bit_words[:, None], shifts[None, :]) & 1  80.7 us
    another operation x12, local copies, waits for them, and re-layouts  38.6 us
  transfers between devices with their start and end apart: 2, of which 1 were waited for; matrix products, arithmetic and copies ran while one was open for 76% of the time, Pallas kernels for 0%

commit v1 on v0

v1 whole, which is shorter than its diff:
```python
import functools
import math

import jax
import jax.numpy as jnp
from jax import lax
from jax.experimental import pallas as pl
from jax.experimental.pallas import tpu as pltpu
from jax.sharding import PartitionSpec as P

BLK = 128
HORIZON = 3.0
BOND_STIFF = 5.0
CONTACT_STIFF = 0.02
CONTACT_DAMP = 0.05
CONTACT_RANGE = 9.0
TIME_STEP = 0.5
VMEM_BYTES = 50 * 1024 * 1024
FAR = 100.0
BOND_UNROLL = 4
PAIR_UNROLL = 4
F32 = jnp.float32
BF16 = jnp.bfloat16


def iota(shape, axis):
    return lax.broadcasted_iota(jnp.int32, shape, axis)


def split3(value):
    one = value.astype(BF16).astype(F32)
    rest = value - one
    two = rest.astype(BF16).astype(F32)
    return one, two, (rest - two).astype(BF16).astype(F32)


def left_rows(value):
    one, two, three = split3(value)
    return jnp.concatenate([one, one, two, one, three, two], axis=0).astype(BF16)


def right_rows(value):
    one, two, three = split3(value)
    return jnp.concatenate([one, two, one, three, one, two], axis=0).astype(BF16)


def dot(left, right, left_dim, right_dim):
    return lax.dot_general(
        left, right, (((left_dim,), (right_dim,)), ((), ())), preferred_element_type=F32
    )


def split2(value):
    high = value.astype(BF16)
    return high, (value - high.astype(F32)).astype(BF16)


def stack_rows(pieces, width):
    row = iota((8, width), 0)
    total = jnp.zeros((8, width), F32)
    for number, piece in pieces.items():
        total = jnp.where(row == number, jnp.broadcast_to(piece, (8, width)), total)
    return total


def lattice_row(node):
    return (
        (node % 8).astype(F32) - 3.5,
        (node // 8 % 8).astype(F32) - 3.5,
        (node // 64).astype(F32) - 5.5,
    )


def pick_kernel(order, shift, velocity, centers, nodes, out, held):
    _, grains, count = shift.shape
    surface = nodes.shape[1]
    blocks = surface // BLK
    owners = out.shape[0]
    share = out.shape[1] // 6
    scale = math.sqrt(2.0 * math.log2(math.e) / CONTACT_RANGE)
    same = iota((grains, grains), 0) == iota((grains, grains), 1)
    offsets = [
        jnp.sum(jnp.where(same, centers[c : c + 1, :], 0.0), axis=1, keepdims=True)
        for c in range(3)
    ]
    for group in range(grains // 8):
        rows = slice(group * 8, group * 8 + 8)
        places = []
        speeds = []
        for tile in range(count // BLK):
            span = slice(tile * BLK, tile * BLK + BLK)
            rest = lattice_row(iota((8, BLK), 1) + tile * BLK)
            now = [rest[c] + shift[c, rows, span] + offsets[c][rows] for c in range(3)]
            places.append([scale * now[c] for c in range(3)])
            speeds.append(
                [
                    CONTACT_STIFF * now[c] - CONTACT_DAMP * velocity[c, rows, span]
                    for c in range(3)
                ]
            )
        for k in range(blocks):
            index = nodes[rows, k * BLK : k * BLK + BLK]
            low = index & (BLK - 1)
            high = index >> 7
            for c in range(6):
                source = places if c < 3 else speeds
                total = jnp.zeros((8, BLK), F32)
                for tile in range(count // BLK):
                    found = jnp.take_along_axis(source[tile][c % 3], low, axis=1)
                    total = jnp.where(high == tile, found, total)
                base = (c * blocks + k) * grains + group * 8
                held[base : base + 8, :] = total

    def send(d, carry):
        for cc in range(share):
            j = order[0, d * share + cc]
            row = (j % blocks) * grains + j // blocks
            for c in range(6):
                out[d, cc * 6 + c : cc * 6 + c + 1, :] = held[
                    pl.ds(row + c * blocks * grains, 1), :
                ]
        return carry

    lax.fori_loop(0, owners, send, 0)


def bond_kernel(tiles, shift, bits, nodes, force, place, lefts, rights, sums, spots, total, radius, square, spread, live):
    _, grains, count = shift.shape
    tile_count = bits.shape[1]
    surface = nodes.shape[1]
    blocks = count // BLK

    q = iota((BLK, BLK), 0)
    p = iota((BLK, BLK), 1)
    flat = (q % 8 - p % 8) ** 2 + (q // 8 % 8 - p // 8 % 8) ** 2
    for delta in range(-2, 3):
        squared = (flat + (2 * delta + q // 64 - p // 64) ** 2).astype(F32)
        kept = (squared > 0.25) & (squared <= HORIZON * HORIZON)
        square[delta + 2] = jnp.where(kept, squared, FAR)
        radius[delta + 2] = jnp.where(kept, jnp.sqrt(squared), 10.0)
    spread[...] = jnp.where(iota((16, BLK), 1) % 16 == iota((16, BLK), 0), 1.0, 0.0).astype(BF16)

    rest = lattice_row(iota((1, count), 1))
    ones = jnp.ones((1, count), F32)

    def prepare(g, carry):
        moved = [shift[c, pl.ds(g, 1), :] for c in range(3)]
        own = sum(2.0 * rest[c] * moved[c] + moved[c] * moved[c] for c in range(3))
        now = [rest[c] + moved[c] for c in range(3)]
        left = stack_rows(
            {0: moved[0], 1: moved[1], 2: moved[2], 3: rest[0], 4: rest[1], 5: rest[2], 6: own, 7: ones},
            count,
        )
        right = stack_rows(
            {
                0: -2.0 * now[0],
                1: -2.0 * now[1],
                2: -2.0 * now[2],
                3: -2.0 * moved[0],
                4: -2.0 * moved[1],
                5: -2.0 * moved[2],
                6: ones,
                7: own,
            },
            count,
        )
        spot = stack_rows({0: now[0], 1: now[1], 2: now[2], 3: ones}, count)
        left_all = left_rows(left)
        right_all = right_rows(right)
        one, two, three = split3(spot)
        sum_all = jnp.concatenate([one, two, three, jnp.zeros_like(one)], axis=0).astype(BF16)
        for h in range(blocks):
            span = slice(h * BLK, h * BLK + BLK)
            at = g * blocks + h
            lefts[at] = left_all[:, span]
            rights[at] = right_all[:, span]
            sums[at, :, :BLK] = sum_all[:, span]
            sums[at, :, BLK:] = sum_all[:, span]
            spots[at] = spot[:, span]
            total[at] = jnp.zeros((8, BLK), F32)

        listed = nodes[pl.ds(g, 1), :]
        low = listed & (BLK - 1)
        high = listed >> 7
        position = iota((1, surface), 1)
        row = iota((8, surface), 0)
        hit = row == jnp.broadcast_to(high, (8, surface))
        first = jnp.where(hit, jnp.broadcast_to((position % BLK + 1).astype(F32), (8, surface)), 0.0)
        second = jnp.where(hit, jnp.broadcast_to((position // BLK).astype(F32), (8, surface)), 0.0)
        chosen = jnp.concatenate([first, second], axis=0).astype(BF16)
        match = jnp.where(
            iota((BLK, surface), 0) == jnp.broadcast_to(low, (BLK, surface)), 1.0, 0.0
        ).astype(BF16)
        found = dot(chosen, match, 1, 1)
        code = (found[:8] + float(BLK) * found[8:]).astype(jnp.int32)
        for h in range(blocks):
            place[pl.ds(h * grains + g, 1), :] = code[h : h + 1, :]
        return carry

    lax.fori_loop(0, grains, prepare, 0)

    def enlist(g, held):
        for t in range(tile_count):
            gap = tiles[2 * t + 1, g] - tiles[2 * t, g]
            live[held] = g * tile_count + t
            held = held + jnp.where((gap <= 2) & (gap >= -2), 1, 0)
        return held

    live_count = lax.fori_loop(0, grains, enlist, 0)
    own_group = (iota((8, BLK), 1) // 16) == iota((8, BLK), 0)
    flag = jnp.left_shift(1, iota((8, BLK), 0))

    def step(n, carry):
        results = []
        for u in range(BOND_UNROLL):
            number = n * BOND_UNROLL + u
            good = number < live_count
            entry = live[jnp.where(good, number, 0)]
            g = entry // tile_count
            t = entry % tile_count
            a = tiles[2 * t, g]
            b = tiles[2 * t + 1, g]
            row_at = g * blocks + a
            col_at = g * blocks + b
            delta = b - a + 2
            excess = dot(lefts[col_at], rights[row_at], 0, 0)
            words = bits[g, pl.ds(t, 1), :].astype(F32)
            sorted_words = jnp.concatenate(
                [
                    jnp.where(
                        own_group,
                        jnp.broadcast_to(words[:, w * BLK : w * BLK + BLK], (8, BLK)),
                        0.0,
                    )
                    for w in range(16)
                ],
                axis=0,
            ).astype(BF16)
            turned = dot(spread[...], sorted_words, 1, 1).astype(jnp.int32)
            rest_square = square[delta]
            now_square = rest_square + excess
            inverse = lax.rsqrt(now_square)
            under = radius[delta] * (now_square * inverse) + rest_square
            bond = excess * inverse / under
            broken = jnp.concatenate(
                [jnp.broadcast_to(turned[w : w + 1], (8, BLK)) & flag for w in range(16)], axis=0
            )
            bond = jnp.where((broken == 0) & (rest_square < 0.5 * FAR), bond, 0.0)
            high, low = split2(bond)
            found = dot(sums[col_at], jnp.concatenate([high, low], axis=0), 1, 0)
            found = found[:8] + found[8:16] + found[16:24]
            gain = BOND_STIFF * (found - spots[row_at] * found[3:4])
            results.append((row_at, jnp.where(good, gain, 0.0)))
        for row_at, gain in results:
            total[row_at] = total[row_at] + gain
        return carry

    lax.fori_loop(0, (live_count + BOND_UNROLL - 1) // BOND_UNROLL, step, 0)

    def finish(g, carry):
        for h in range(blocks):
            for c in range(3):
                force[pl.ds((c * blocks + h) * grains + g, 1), :] = total[g * blocks + h, c : c + 1, :]
        return carry

    lax.fori_loop(0, grains, finish, 0)


def contact_kernel(pairs, count, received, out, lefts, rights, sums, total):
    owners = received.shape[0]
    share = received.shape[1] // 6

    def prepare(s, carry):
        for cc in range(share):
            at = s * share + cc
            line = [received[s, cc * 6 + c : cc * 6 + c + 1, :] for c in range(6)]
            own = -0.5 * (line[0] * line[0] + line[1] * line[1] + line[2] * line[2])
            one = jnp.ones((1, BLK), F32)
            base = {0: line[0], 1: line[1], 2: line[2]}
            lefts[at] = left_rows(stack_rows({**base, 3: own, 4: one}, BLK))
            rights[at] = right_rows(stack_rows({**base, 3: one, 4: own}, BLK))
            first, second, _ = split3(stack_rows({0: line[3], 1: line[4], 2: line[5], 3: one}, BLK))
            both = jnp.concatenate([first, second], axis=0).astype(BF16)
            sums[at, :, :BLK] = both
            sums[at, :, BLK:] = both
            total[at] = jnp.zeros((8, BLK), F32)
        return carry

    lax.fori_loop(0, owners, prepare, 0)
    live = count[0]

    def step(n, carry):
        results = []
        for u in range(PAIR_UNROLL):
            number = n * PAIR_UNROLL + u
            good = number < live
            at = jnp.where(good, number, 0)
            i = pairs[0, at]
            j = pairs[1, at]
            weight = jnp.exp2(dot(lefts[j], rights[i], 0, 0))
            high, low = split2(weight)
            gain_i = dot(sums[j], jnp.concatenate([high, low], axis=0), 1, 0)
            gain_j = dot(sums[i], jnp.concatenate([high, low], axis=1), 1, 1)
            results.append((i, jnp.where(good, gain_i[:8] + gain_i[8:], 0.0)))
            results.append((j, jnp.where(good, gain_j[:8] + gain_j[8:], 0.0)))
        for at, gain in results:
            total[at] = total[at] + gain
        return carry

    lax.fori_loop(0, (live + PAIR_UNROLL - 1) // PAIR_UNROLL, step, 0)

    def finish(s, carry):
        for cc in range(share):
            found = total[s * share + cc]
            weight = found[3:4]
            for c in range(3):
                out[s, cc * 3 + c : cc * 3 + c + 1, :] = (
                    received[s, cc * 6 + 3 + c : cc * 6 + 4 + c, :] * weight - found[c : c + 1]
                )
        return carry

    lax.fori_loop(0, owners, finish, 0)


def finish_kernel(order, returned, place, bond, velocity, force, speed, held):
    _, grains, count = velocity.shape
    owners = returned.shape[0]
    node_blocks = count // BLK
    share = returned.shape[1] // 3
    blocks = held.shape[0] // (3 * grains)

    def accept(d, carry):
        for cc in range(share):
            j = order[0, d * share + cc]
            row = (j % blocks) * grains + j // blocks
            for c in range(3):
                held[pl.ds(row + c * blocks * grains, 1), :] = returned[
                    d, cc * 3 + c : cc * 3 + c + 1, :
                ]
        return carry

    lax.fori_loop(0, owners, accept, 0)
    for group in range(grains // 8):
        rows = slice(group * 8, group * 8 + 8)
        for tile in range(count // BLK):
            span = slice(tile * BLK, tile * BLK + BLK)
            base = tile * grains + group * 8
            code = place[base : base + 8, :]
            spot = code - 1
            low = spot & (BLK - 1)
            high = jnp.where(code == 0, -1, spot >> 7)
            for c in range(3):
                total = jnp.zeros((8, BLK), F32)
                for k in range(blocks):
                    at = (c * blocks + k) * grains + group * 8
                    found = jnp.take_along_axis(held[at : at + 8, :], low, axis=1)
                    total = jnp.where(high == k, found, total)
                near = (c * node_blocks + tile) * grains + group * 8
                total = bond[near : near + 8, :] + total
                force[c, rows, span] = total
                speed[c, rows, span] = velocity[c, rows, span] + TIME_STEP * total


def on_device(displacement, velocity, centers, tile_list, broken_bits, surface_nodes, send_order, pair_list, pair_count):
    grains, _, count = displacement.shape
    owners = lax.axis_size("grain") * lax.axis_size("cell")
    slots = send_order.shape[1]
    share = slots // owners
    surface = surface_nodes.shape[1]
    blocks = surface // BLK
    node_blocks = count // BLK
    tile_count = tile_list.shape[1]
    shift = displacement.transpose(1, 0, 2)
    speed = velocity.transpose(1, 0, 2)
    tiles = tile_list.transpose(1, 2, 0).reshape(2 * tile_count, grains)
    pairs = pair_list[0].T
    vmem = pl.BlockSpec(memory_space=pltpu.VMEM)
    smem = pl.BlockSpec(memory_space=pltpu.SMEM)
    params = pltpu.CompilerParams(vmem_limit_bytes=VMEM_BYTES)

    outgoing = pl.pallas_call(
        pick_kernel,
        out_shape=jax.ShapeDtypeStruct((owners, 6 * share, BLK), F32),
        in_specs=[smem, vmem, vmem, vmem, vmem],
        out_specs=vmem,
        scratch_shapes=[pltpu.VMEM((6 * slots, BLK), F32)],
        compiler_params=params,
        name="pick",
    )(send_order, shift, speed, centers, surface_nodes)

    received = lax.all_to_all(outgoing, ("grain", "cell"), split_axis=0, concat_axis=0, tiled=True)

    bond, place = pl.pallas_call(
        bond_kernel,
        out_shape=(
            jax.ShapeDtypeStruct((3 * node_blocks * grains, BLK), F32),
            jax.ShapeDtypeStruct((node_blocks * grains, BLK), jnp.int32),
        ),
        in_specs=[smem, vmem, vmem, vmem],
        out_specs=(vmem, vmem),
        scratch_shapes=[
            pltpu.VMEM((grains * node_blocks, 48, BLK), BF16),
            pltpu.VMEM((grains * node_blocks, 48, BLK), BF16),
            pltpu.VMEM((grains * node_blocks, 32, 2 * BLK), BF16),
            pltpu.VMEM((grains * node_blocks, 8, BLK), F32),
            pltpu.VMEM((grains * node_blocks, 8, BLK), F32),
            pltpu.VMEM((5, BLK, BLK), F32),
            pltpu.VMEM((5, BLK, BLK), F32),
            pltpu.VMEM((16, BLK), BF16),
            pltpu.SMEM((grains * tile_count + 1,), jnp.int32),
        ],
        compiler_params=params,
        cost_estimate=pl.CostEstimate(flops=4_000_000_000, bytes_accessed=3_000_000, transcendentals=4_000_000),
        name="bond",
    )(tiles, shift, broken_bits, surface_nodes)

    slot_force = pl.pallas_call(
        contact_kernel,
        out_shape=jax.ShapeDtypeStruct((owners, 3 * share, BLK), F32),
        in_specs=[smem, smem, vmem],
        out_specs=vmem,
        scratch_shapes=[
            pltpu.VMEM((slots, 48, BLK), BF16),
            pltpu.VMEM((slots, 48, BLK), BF16),
            pltpu.VMEM((slots, 16, 2 * BLK), BF16),
            pltpu.VMEM((slots, 8, BLK), F32),
        ],
        compiler_params=params,
        name="contact",
    )(pairs, pair_count, received)

    returned = lax.all_to_all(slot_force, ("grain", "cell"), split_axis=0, concat_axis=0, tiled=True)

    force, new_speed = pl.pallas_call(
        finish_kernel,
        out_shape=(jax.ShapeDtypeStruct((3, grains, count), F32),) * 2,
        in_specs=[smem, vmem, vmem, vmem, vmem],
        out_specs=(vmem, vmem),
        scratch_shapes=[pltpu.VMEM((3 * slots, BLK), F32)],
        compiler_params=params,
        name="finish",
    )(send_order, returned, place, bond, speed)
    return force.transpose(1, 0, 2), new_speed.transpose(1, 0, 2)


def solution(mesh):
    own = ("grain", "cell")
    return jax.shard_map(
        on_device,
        mesh=mesh,
        in_specs=(
            P(own, None, None),
            P(own, None, None),
            P(None, own),
            P(own, None, None),
            P(own, None, None),
            P(own, None),
            P(own, None),
            P(own, None, None),
            P(own),
        ),
        out_specs=(P(own, None, None), P(own, None, None)),
        check_vma=False,
    )
```

time: 1900 us -> 89 us (0.05)
  the two profiles are of different devices: /device:TPU:1 before, /device:TPU:9 now
where the time goes in v1:
time: 89 us; the launch traced here: 87.8 us
  Pallas kernels  61.6 us (69%)
  waiting for transfers between devices  10.8 us (12%)
  starting transfers between devices  10.5 us (12%)
  local copies, waits for them, and re-layouts  3.46 us (4%)
  between operations  1.39 us (2%)
    pallas_call x1, Pallas kernels, on_device(): pl.pallas_call(bond_kernel, out_shape=(jax.ShapeDtypeStruct((3 * node_blo...  32.1 us
    pallas_call x1, Pallas kernels, on_device(): pl.pallas_call(contact_kernel, out_shape=jax.ShapeDtypeStruct((owners, 3...  23.5 us
    all_to_all x1, waiting for transfers between devices, on_device(): lax.all_to_all(outgoing, ('grain', 'cell'), split_axis=0, concat_axis=0,...  10.8 us
    all_to_all x1, starting transfers between devices, on_device(): lax.all_to_all(outgoing, ('grain', 'cell'), split_axis=0, concat_axis=0,...  6.36 us
    all_to_all x1, starting transfers between devices, on_device(): lax.all_to_all(slot_force, ('grain', 'cell'), split_axis=0, concat_axis=0...  4.19 us
    unnamed x22, local copies, waits for them, and re-layouts  3.46 us
    pallas_call x1, Pallas kernels, on_device(): pl.pallas_call(pick_kernel, out_shape=jax.ShapeDtypeStruct((owners, 6 * s...  3.19 us
    pallas_call x1, Pallas kernels, on_device(): pl.pallas_call(finish_kernel, out_shape=(jax.ShapeDtypeStruct((3, grains,...  2.81 us
  transfers between devices with their start and end apart: 2, of which 1 were waited for; matrix products, arithmetic and copies ran while one was open for 0% of the time, Pallas kernels for 37%

profile of v1, /device:TPU:9, one launch (start us, length us, event | category | flops | bytes accessed | tf_op | source)
XLA Modules:
  0.0 87.8 jit_solution(5504840662160173716)
XLA Ops:
  0.6 0.0 copy-start.7
  0.6 0.0 copy-start.6
  0.7 0.7 copy-done.7
  1.3 0.0 copy-done.6
  1.3 0.0 copy-start
  1.3 1.0 %copy-done = f32[32,3,768]{2,0,1:T(8,128)S(1)} copy-done((f32[32,3,768]{2,0,1:T(8,128)S(1)}, f32[32,3,768]{2,0,1:T(8,128)}, u32[]{:S(2)}) %copy-start) | copy-done | bytes 294936
  2.3 1.0 %copy-done.2 = f32[32,3,768]{2,0,1:T(8,128)S(1)} copy-done((f32[32,3,768]{2,0,1:T(8,128)S(1)}, f32[32,3,768]{2,0,1:T(8,128)}, u32[]{:S(2)}) %copy-start.2) | copy-done | bytes 294936
  3.2 0.8 copy-done.4
  4.1 3.2 %pick.1 = f32[32,24,128]{2,1,0:T(8,128)} custom-call(s32[1,128]{1,0:T(1,128)S(1)} %copy-done.6, f32[3,32,768]{2,1,0:T(8,128)S(1)} %bitcast.12, f32[3,32,768]{2,1,0:T(8,128)S(1)} %bitcast.10, f32[3,32]{1,0:T(4,128)S(1)} %copy-done.7, s32[32,512]{1,0:T(8,128)S(1)} %copy-done.4), custom_call_target="tpu_custom_call" | custom-call | tf_op jit(solution)/shard_map/pick/pallas_call | solution.py:381
  7.3 6.4 %all-to-all-start = ((f32[32,24,128]{2,1,0:T(8,128)}), f32[32,24,128]{2,1,0:T(8,128)S(1)}, u32[]{:S(2)}, u32[]{:S(2)}) async-start(f32[32,24,128]{2,1,0:T(8,128)} %pick.1), calls=%async_computation | async-start | bytes 786432 | tf_op jit(solution)/shard_map/all_to_all | solution.py:391
  14.3 0.0 copy-start.8
  14.3 10.8 %all-to-all-done.received = f32[32,24,128]{2,1,0:T(8,128)S(1)} async-done(((f32[32,24,128]{2,1,0:T(8,128)}), f32[32,24,128]{2,1,0:T(8,128)S(1)}, u32[]{:S(2)}, u32[]{:S(2)}) %all-to-all-start) | async-done | bytes 393248 | tf_op jit(solution)/shard_map/all_to_all | solution.py:391
  25.1 0.0 copy-done.8
  25.1 23.5 %contact.1 = f32[32,12,128]{2,1,0:T(8,128)} custom-call(s32[2,128]{1,0:T(2,128)S(1)} %bitcast.14, s32[1]{0:T(128)S(6)} %copy.11.count, f32[32,24,128]{2,1,0:T(8,128)S(1)} %all-to-all-done.received), custom_call_target="tpu_custom_call" | custom-call | tf_op jit(solution)/shard_map/contact/pallas_call | solution.py:417
  48.6 4.2 %all-to-all-start.1 = ((f32[32,12,128]{2,1,0:T(8,128)}), f32[32,12,128]{2,1,0:T(8,128)S(1)}, u32[]{:S(2)}, u32[]{:S(2)}) async-start(f32[32,12,128]{2,1,0:T(8,128)} %contact.1), calls=%async_computation.1 | async-start | bytes 524288 | tf_op jit(solution)/shard_map/all_to_all | solution.py:432
  52.8 0.0 copy-done.9
  52.8 0.0 copy-done.3
  52.8 0.0 copy-done.5
  52.8 0.0 copy-done.10
  52.8 0.0 copy-start.1
  52.8 32.1 %bond.1 = (f32[576,128]{1,0:T(8,128)S(1)}, s32[192,128]{1,0:T(8,128)S(1)}) custom-call(s32[8,32]{1,0:T(8,128)S(1)} %bitcast.15, f32[3,32,768]{2,1,0:T(8,128)S(1)} %bitcast.13, s32[32,4,2048]{2,1,0:T(4,128)S(1)} %copy-done.9, s32[32,512]{1,0:T(8,128)S(1)} %copy-done.5), custom_call_target="tpu_custom_call" | custom-call | flops 4000000000 | bytes 3000000 | tf_op jit(solution)/shard_map/bond/pallas_call | solution.py:393
  84.9 0.0 all-to-all-done.1.returned
  84.9 0.0 copy-done.1
  84.9 2.8 %finish.1 = (f32[3,32,768]{2,1,0:T(8,128)}, f32[3,32,768]{2,1,0:T(8,128)}) custom-call(s32[1,128]{1,0:T(1,128)S(1)} %copy-done.6, f32[32,12,128]{2,1,0:T(8,128)S(1)} %all-to-all-done.1.returned, s32[192,128]{1,0:T(8,128)S(1)} %get-tuple-element.6.place, f32[576,128]{1,0:T(8,128)S(1)} %get-tuple-element.7.bond, f32[3,32,768]{2,1,0:T(8,128)S(1)} %bitcast.11), custom_call_target="tpu_custom_call" | custom-call | tf_op jit(solution)/shard_map/finish/pallas_call | solution.py:434
  (6 shorter events, 0.0 us)
Async XLA Ops:
  0.6 0.7 copy-start.7
  0.6 0.7 copy-start.6
  1.3 1.0 %copy-start = (f32[32,3,768]{2,0,1:T(8,128)S(1)}, f32[32,3,768]{2,0,1:T(8,128)}, u32[]{:S(2)}) copy-start(f32[32,3,768]{2,0,1:T(8,128)} %param.10) | copy-start | bytes 884740
  2.3 1.0 %copy-start.2 = (f32[32,3,768]{2,0,1:T(8,128)S(1)}, f32[32,3,768]{2,0,1:T(8,128)}, u32[]{:S(2)}) copy-start(f32[32,3,768]{2,0,1:T(8,128)} %param.9) | copy-start | bytes 884740
  3.2 0.8 copy-start.4
  4.1 48.7 %copy-start.9 = (s32[32,4,2048]{2,1,0:T(4,128)S(1)}, s32[32,4,2048]{2,1,0:T(4,128)}, u32[]{:S(2)}) copy-start(s32[32,4,2048]{2,1,0:T(4,128)} %bits.1) | copy-start | bytes 3145732
  7.3 17.8 %all-to-all-start = ((f32[32,24,128]{2,1,0:T(8,128)}), f32[32,24,128]{2,1,0:T(8,128)S(1)}, u32[]{:S(2)}, u32[]{:S(2)}) async-start(f32[32,24,128]{2,1,0:T(8,128)} %pick.1), calls=%async_computation | async-start | bytes 786432 | tf_op jit(solution)/shard_map/all_to_all | solution.py:391
  14.3 10.8 %copy-start.8 = (s32[1,128,2]{1,2,0:T(2,128)S(1)}, s32[1,128,2]{1,2,0:T(2,128)}, u32[]{:S(2)}) copy-start(s32[1,128,2]{1,2,0:T(2,128)} %param.16) | copy-start | bytes 3076
  48.6 4.2 %copy-start.3 = (f32[32,3,768]{2,0,1:T(8,128)S(1)}, f32[32,3,768]{2,0,1:T(8,128)}, u32[]{:S(2)}) copy-start(f32[32,3,768]{2,0,1:T(8,128)} %param.9) | copy-start | bytes 884740
  48.6 4.2 %copy-start.5 = (s32[32,512]{1,0:T(8,128)S(1)}, s32[32,512]{1,0:T(8,128)}, u32[]{:S(2)}) copy-start(s32[32,512]{1,0:T(8,128)} %nodes.3) | copy-start | bytes 196612
  48.6 4.2 %copy-start.10 = (s32[32,4,2]{0,2,1:T(2,128)S(1)}, s32[32,4,2]{0,2,1:T(2,128)}, u32[]{:S(2)}) copy-start(s32[32,4,2]{0,2,1:T(2,128)} %param.12) | copy-start | bytes 3076
  48.6 36.4 %all-to-all-start.1 = ((f32[32,12,128]{2,1,0:T(8,128)}), f32[32,12,128]{2,1,0:T(8,128)S(1)}, u32[]{:S(2)}, u32[]{:S(2)}) async-start(f32[32,12,128]{2,1,0:T(8,128)} %contact.1), calls=%async_computation.1 | async-start | bytes 524288 | tf_op jit(solution)/shard_map/all_to_all | solution.py:432
  52.8 32.1 %copy-start.1 = (f32[32,3,768]{2,0,1:T(8,128)S(1)}, f32[32,3,768]{2,0,1:T(8,128)}, u32[]{:S(2)}) copy-start(f32[32,3,768]{2,0,1:T(8,128)} %param.10) | copy-start | bytes 884740
